TPU v7x, 32 devices: a whole 2x2x4 slice. The times are simulated.
32 devices in a mesh: section: 16 (over z, y, x), rep: 2 (over core).
Axes of the slice: x: 2, y: 2, z: 4, core: 2. Of those that a mesh axis runs over, the one named last changes fastest.
Arguments:
- features: bfloat16 [4096, 512], P(('section', 'rep')), may hold values from -6 to 6
- col_panels: int32 [32, 2, 12], P('section', 'rep'), may hold values from 0 to 31, as said below
- block_counts: int32 [32, 2], P('section', 'rep'), may hold values from 1 to 12, as said below
- block_values: bfloat16 [32, 2, 12, 128, 128], P('section', 'rep'), may hold values from 0.0019989014 to 0.019897461
- weight: bfloat16 [512, 512], replicated, may hold values from -0.25 to 0.25
- bias: float32 [512], replicated, may hold values from -3 to 3
- cotangent: bfloat16 [4096, 512], P(('section', 'rep')), may hold values from -6 to 6
Outputs:
- hidden: bfloat16 [4096, 512], P(('section', 'rep'))
- weight_grad: float32 [512, 512], replicated
- bias_grad: float32 [512], replicated
Inputs may be any that keep to these rules, and one draw needn't show every extreme that they name: Column group r holds the column panels c with (c) % 2 == r; col_panels[p, r, k] lies in column group r, and the 12 entries of one list are distinct. Only the first block_counts[p, r] slots of a list are nonzero blocks; later slots are ignored. The count 12 occurs in every draw.
All inputs are finite; a program needn't handle non-finite values.
Results may differ from a plain program's by a relative error of at most 0.0055.
Values may be sent and summed in bfloat16 or wider, within the bound.
A program may use at most 64 MiB of HBM per device.

v0:
```python
import math

import jax
import jax.numpy as jnp
from jax import lax
from jax.sharding import PartitionSpec as P


def shards(features, col_panels, block_counts, block_values, weight, bias, cotangent):
    rep_count = lax.axis_size("rep")
    rep_index = lax.axis_index("rep")
    tile_size = block_values.shape[-1]
    feat_width = features.shape[1]
    own_panels = features.shape[0] // tile_size
    row_panels = col_panels.shape[0]
    slot_count = col_panels.shape[2]
    global_cols = col_panels[:, 0, :]
    local_cols = global_cols // (own_panels * rep_count) * own_panels + global_cols % own_panels
    live_counts = block_counts[:, 0]
    slot_mask = jnp.arange(slot_count, dtype=jnp.int32)[None, :] < live_counts[:, None]
    tiles = block_values[:, 0]
    empty = jnp.zeros((row_panels, tile_size, feat_width), jnp.float32)
    gathered = lax.all_gather(features, "section", axis=0, tiled=True)
    all_panels = gathered.reshape(-1, tile_size, feat_width)
    slot_step = 4
    turn_count = (jnp.max(live_counts) + slot_step - 1) // slot_step

    def one_turn(turn, running):
        begin_slot = turn * slot_step
        step_cols = lax.dynamic_slice_in_dim(local_cols, begin_slot, slot_step, 1)
        step_mask = lax.dynamic_slice_in_dim(slot_mask, begin_slot, slot_step, 1)
        step_tiles = lax.dynamic_slice_in_dim(tiles, begin_slot, slot_step, 1)
        step_tiles = jnp.where(step_mask[:, :, None, None], step_tiles, jnp.zeros((), jnp.bfloat16))
        picked = all_panels[step_cols]
        return running + jnp.einsum(
            "gkab,gkbf->gaf", step_tiles, picked, preferred_element_type=jnp.float32
        )

    gathered_sum = lax.fori_loop(0, turn_count, one_turn, empty)
    partial_value = gathered_sum.reshape(row_panels * tile_size, feat_width)
    own_rows = own_panels * tile_size
    summed_all = lax.psum(partial_value, "rep")
    summed_own = lax.dynamic_slice_in_dim(summed_all, rep_index * own_rows, own_rows, 0)
    aggregated = summed_own.astype(jnp.bfloat16)
    pre = jnp.dot(aggregated, weight, preferred_element_type=jnp.float32) + bias
    hidden = jax.nn.silu(pre).astype(jnp.bfloat16)
    sigmoid_pre = jax.nn.sigmoid(pre)
    slope = (
        cotangent.astype(jnp.float32) * (sigmoid_pre * (1.0 + pre * (1.0 - sigmoid_pre)))
    ).astype(jnp.bfloat16)
    local_weight = jnp.einsum("nd,nf->df", aggregated, slope, preferred_element_type=jnp.float32)
    local_bias = jnp.sum(slope.astype(jnp.float32), axis=0)
    weight_sum, bias_sum = lax.psum((local_weight, local_bias), ("section", "rep"))
    node_total = lax.axis_size("section") * rep_count * own_rows
    factor = 1.0 / math.sqrt(node_total)
    return (hidden, weight_sum * factor, bias_sum * factor)


def solution(mesh):
    in_specs = (
        P(("section", "rep"), None),
        P("section", "rep", None),
        P("section", "rep"),
        P("section", "rep", None, None, None),
        P(),
        P(),
        P(("section", "rep"), None),
    )
    out_specs = (P(("section", "rep"), None), P(), P())
    return jax.shard_map(shards, mesh=mesh, in_specs=in_specs, out_specs=out_specs, check_vma=False)
```

profile of v0, /device:TPU:0, one launch (start us, length us, event | category | flops | bytes accessed | tf_op | source)
XLA Modules:
  0.0 230.5 jit_solution(8685731032697986386)
XLA Ops:
  7.2 0.7 all-gather.2.cloned.1.call-update
  8.0 1.3 reduce_max.9
  9.9 0.7 iota_compare_fusion
  10.7 0.7 and_select_fusion
  11.3 62.9 %all-gather.2.cloned.1.call-done = bf16[2048,512]{1,0:T(8,128)(2,1)} async-done(((bf16[128,512]{1,0:T(8,128)(2,1)}), bf16[2048,512]{1,0:T(8,128)(2,1)}) %all-gather.2.cloned.1.call-update) | async-done | bytes 2097168 | tf_op jit(solution)/shard_map/all_gather | solution.py:23
  74.3 11.4 %while.10 = (s32[]{:T(128)}, f32[2,128,512]{2,1,0:T(8,128)S(1)}, s32[]{:T(128)}, pred[2,12]{1,0:T(4,128)(4,1)S(1)}, bf16[2,12,128,128]{3,2,1,0:T(8,128)(2,1)}, /...) while((s32[]{:T(128)}, f32[2,128,512]{2,1,0:T(8,128)S(1)}, ...), condition=%wide.region_2.3_spmd, body=%wide.region_1.2_spmd.sunk | while | flops 134480928 | bytes 4460927 | solution.py:39
  74.4 0.1 reshape.32
  74.5 2.2 gather_fusion
  76.7 0.1 constant_dynamic-slice_fusion.2
  76.8 1.3 fusion.18
  78.2 0.1 reshape.32
  78.3 2.2 gather_fusion
  80.5 0.1 constant_dynamic-slice_fusion.2
  80.6 1.3 fusion.18
  82.0 0.1 reshape.32
  82.1 2.2 gather_fusion
  84.4 1.3 fusion.18
  85.7 4.8 %all-reduce.4 = bf16[256,512]{1,0:T(8,128)(2,1)S(1)} all-reduce(f32[256,512]{1,0:T(8,128)S(1)} %bitcast.21), channel_id=1, replica_groups=mesh['section'=16,'rep'=2] {'rep'}, use_global_device_ids=true, to_apply=%region_3.4 | all-reduce | flops 131072 | bytes 786432 | tf_op jit(solution)/shard_map/psum | solution.py:42
  90.6 1.0 convert_reduce_fusion
  91.6 1.3 fusion.7
  92.9 38.5 %psum.23 = f32[512]{0:T(512)S(1)} all-reduce(f32[512]{0:T(512)S(1)} %get-tuple-element.56), channel_id=1, replica_groups=mesh['section'=16,'rep'=2] {'section','rep'}, use_global_device_ids=true, to_apply=%region_6.7 | all-reduce | flops 512 | bytes 4096 | tf_op jit(solution)/shard_map/psum | solution.py:53
  131.4 0.6 broadcast_multiply_fusion.1
  132.0 89.3 %all-reduce.3.cloned.1.call-done = f32[512,512]{1,0:T(8,128)} async-done(((f32[512,512]{1,0:T(8,128)}), f32[512,512]{1,0:T(8,128)}) %all-reduce.3.cloned.1.call-update) | async-done | bytes 1048592 | tf_op jit(solution)/shard_map/psum | solution.py:53
  221.3 2.3 broadcast_multiply_fusion
  (17 shorter events, 0.5 us)
Async XLA Ops:
  7.2 83.4 %copy-start = (bf16[512,512]{1,0:T(8,128)(2,1)S(1)}, bf16[512,512]{1,0:T(8,128)(2,1)}, u32[]{:S(2)}) copy-start(bf16[512,512]{1,0:T(8,128)(2,1)} %param.13) | copy-start | bytes 1572868
  7.2 67.0 %all-gather.2.cloned.1.call-start = ((), (), s32[]{:S(2)}) async-start(), calls=%async_computation | async-start | bytes 2228224 | tf_op jit(solution)/shard_map/all_gather | solution.py:23
  7.9 213.4 %all-reduce.3.cloned.1.call-start = ((), (), s32[]{:S(2)}) async-start(), calls=%async_computation.1 | async-start | bytes 2097152 | tf_op jit(solution)/shard_map/psum | solution.py:53
  74.3 16.3 %copy-start.1 = (bf16[128,512]{1,0:T(8,128)(2,1)S(1)}, bf16[128,512]{1,0:T(8,128)(2,1)}, u32[]{:S(2)}) copy-start(bf16[128,512]{1,0:T(8,128)(2,1)} %param.15) | copy-start | bytes 393220
  74.3 16.3 %copy-start.2 = (f32[512]{0:T(512)S(1)}, f32[512]{0:T(512)}, u32[]{:S(2)}) copy-start(f32[512]{0:T(512)} %param.14) | copy-start | bytes 6148
Sparse Core Ops, SparseCore 0:
  10.8 63.3 all-gather.1
  93.0 128.2 all-reduce.2
where the time goes:
time: 231 us; the launch traced here: 230 us
  waiting for transfers between devices  153 us (66%)
  blocking collectives  43.4 us (19%)
  between operations  14.8 us (6%)
  local copies, waits for them, and re-layouts  7.17 us (3%)
  matrix products  6.22 us (3%)
  other arithmetic  5.83 us (3%)
    psum x1, waiting for transfers between devices, shards(): lax.psum((local_weight, local_bias), ('section', 'rep'))  89.3 us
    all_gather x1, waiting for transfers between devices, shards(): gathered = lax.all_gather(features, 'section', axis=0, tiled=True)  62.9 us
    psum x1, blocking collectives, shards(): lax.psum((local_weight, local_bias), ('section', 'rep'))  38.5 us
    gather x3, local copies, waits for them, and re-layouts, one_turn(): picked = all_panels[step_cols]  6.61 us
    psum x1, blocking collectives, shards(): summed_all = lax.psum(partial_value, 'rep')  4.82 us
  transfers between devices with their start and end apart: 2, of which 2 were waited for; matrix products, arithmetic and copies ran while one was open for 1% of the time, Pallas kernels for 0%

commit v1 on v0

--- a/solution.py
+++ b/solution.py
@@ -3,6 +3,8 @@
 import jax
 import jax.numpy as jnp
 from jax import lax
+from jax.experimental import pallas as pl
+from jax.experimental.pallas import tpu as pltpu
 from jax.sharding import PartitionSpec as P
 
 
@@ -55,6 +57,297 @@
     factor = 1.0 / math.sqrt(node_total)
     return (hidden, weight_sum * factor, bias_sum * factor)
 
+MESH = pl.DeviceIdType.MESH
+Z, PLANE = 4, 4
+
+
+def fused_kernel(
+    feat, cols, counts, blocks, weight, bias, cot,
+    hid_out, wg_out, bias_out,
+    gath, dense, blk, wv, cotv, acc_own, acc_oth, acc_in, aggs, hidv,
+    pair_out, pair_in, half32, half16, plane_in, sum32, sum16, line_in, fin,
+    ext, ext_pair, ext_plane, ext_line,
+    loc_sem, z_s, z_r, x_s, x_r, y_s, y_r, dx_s, dx_r, dy_s, dy_r,
+    p_s, p_r, rs_s, rs_r, zl_s, zl_r, zg_s, zg_r, pg_s, pg_r, cg_s, cg_r,
+):
+    tile, width = feat.shape
+    slots = cols.shape[2]
+    me, rep = lax.axis_index("section"), lax.axis_index("rep")
+    z, q = me // PLANE, me % PLANE
+    y, x = q // 2, q % 2
+
+    def flip(j):
+        return (1 - y if j & 2 else y) * 2 + (1 - x if j & 1 else x)
+
+    def line(d):
+        return lax.rem(z + d, Z)
+
+    plane_peer = {j: (z * PLANE + flip(j), rep) for j in (1, 2, 3)}
+    line_peer = {d: (line(d) * PLANE + q, rep) for d in (1, 2, 3)}
+    core_peer = (me, 1 - rep)
+
+    def remote(src, dst, send, recv, peer):
+        return pltpu.make_async_remote_copy(
+            src_ref=src, dst_ref=dst, send_sem=send, recv_sem=recv,
+            device_id=peer, device_id_type=MESH,
+        )
+
+    own = gath.at[0, pl.ds(0, tile)]
+    load_feat = pltpu.make_async_copy(feat, own, loc_sem.at[0])
+    load_blk = pltpu.make_async_copy(blocks, blk, loc_sem.at[1])
+    load_w = pltpu.make_async_copy(weight, wv, loc_sem.at[2])
+    load_cot = pltpu.make_async_copy(cot, cotv, loc_sem.at[3])
+    for c in (load_feat, load_blk, load_w, load_cot):
+        c.start()
+
+    barrier = pltpu.get_barrier_semaphore()
+    peers = list(plane_peer.values()) + list(line_peer.values()) + [core_peer]
+    for peer in peers:
+        pl.semaphore_signal(barrier, inc=1, device_id=peer, device_id_type=MESH)
+    pl.semaphore_wait(barrier, len(peers))
+    load_feat.wait()
+
+    def slot(j, k):
+        return gath.at[j, pl.ds(k * tile, tile)]
+
+    def half(j, k, h):
+        return gath.at[j, pl.ds(k * tile + h * (tile // 2), tile // 2)]
+
+    z_copy = {
+        d: remote(slot(0, 0), slot(0, Z - d), z_s.at[d], z_r.at[Z - d], line_peer[d])
+        for d in (1, 2, 3)
+    }
+    x_copy = {k: remote(slot(0, k), slot(1, k), x_s.at[k], x_r.at[k], plane_peer[1]) for k in range(Z)}
+    y_copy = {k: remote(slot(0, k), slot(2, k), y_s.at[k], y_r.at[k], plane_peer[2]) for k in range(Z)}
+    dx_copy = {k: remote(half(2, k, 0), half(3, k, 0), dx_s.at[k], dx_r.at[k], plane_peer[1]) for k in range(Z)}
+    dy_copy = {k: remote(half(1, k, 1), half(3, k, 1), dy_s.at[k], dy_r.at[k], plane_peer[2]) for k in range(Z)}
+
+    for d in (1, 3, 2):
+        z_copy[d].start()
+    x_copy[0].start()
+    y_copy[0].start()
+
+    load_blk.wait()
+
+    def build(j):
+        for k in range(Z):
+            column = (line(k) * PLANE + flip(j)) * 2 + rep
+            for p in range(2):
+                panel = rep if p == 0 else 1 - rep
+                found = jnp.int32(-1)
+                for s in range(slots):
+                    hit = jnp.logical_and(cols[panel, 0, s] == column, s < counts[panel, 0])
+                    found = jnp.where(hit, jnp.int32(s), found)
+                block = blk[panel, 0, jnp.maximum(found, 0)]
+                keep = (found >= 0).astype(jnp.float32).astype(jnp.bfloat16)
+                dense[j, pl.ds(p * tile, tile), pl.ds(k * tile, tile)] = block * keep
+
+    for j in range(2):
+        build(j)
+    by_arrival = (1, 3, 2)
+
+    def forward(k):
+        x_copy[k].wait_recv()
+        dy_copy[k].start()
+        y_copy[k].wait_recv()
+        dx_copy[k].start()
+
+    for k in by_arrival:
+        z_copy[Z - k].wait_recv()
+        x_copy[k].start()
+        y_copy[k].start()
+        if k == 1:
+            forward(0)
+    build(2)
+    build(3)
+    rows = pl.ds(0, 2 * tile)
+    mine, theirs = pl.ds(0, tile), pl.ds(tile, tile)
+
+    def product(j, part):
+        return jnp.dot(dense[j, part], gath[j], preferred_element_type=jnp.float32)
+
+    acc_own[...] = product(0, mine)
+    acc_oth[...] = product(0, theirs)
+    for k in by_arrival:
+        forward(k)
+    for j in (1, 2):
+        acc_own[...] += product(j, mine)
+        acc_oth[...] += product(j, theirs)
+    for k in (0,) + by_arrival:
+        dx_copy[k].wait_recv()
+        dy_copy[k].wait_recv()
+    acc_oth[...] += product(3, theirs)
+    swap = remote(acc_oth, acc_in, p_s.at[0], p_r.at[0], core_peer)
+    swap.start()
+    acc_own[...] += product(3, mine)
+    load_w.wait()
+    load_cot.wait()
+    swap.wait()
+
+    agg = (acc_own[...] + acc_in[...]).astype(jnp.bfloat16)
+    aggs[...] = agg
+    pre = jnp.dot(agg, wv[...], preferred_element_type=jnp.float32) + bias[...]
+    sig = jax.nn.sigmoid(pre)
+    slope = (cotv[...].astype(jnp.float32) * (sig * (1.0 + pre * (1.0 - sig)))).astype(jnp.bfloat16)
+    half_rows = width // 2
+
+    def grad_half(which):
+        part = aggs[:, pl.ds(pl.multiple_of(which * half_rows, half_rows), half_rows)]
+        return lax.dot_general(part, slope, (((0,), (0,)), ((), ())), preferred_element_type=jnp.float32)
+
+    pair_out[...] = grad_half(1 - rep).astype(jnp.bfloat16)
+    pair = remote(pair_out, pair_in, p_s.at[1], p_r.at[1], core_peer)
+    pair.start()
+    total = jnp.sum(slope.astype(jnp.float32), axis=0, keepdims=True)
+    lanes = width // 4
+    row_id = lax.broadcasted_iota(jnp.int32, (8, lanes), 0)
+    spread = jnp.zeros((8, lanes), jnp.float32)
+    for i in range(4):
+        spread = jnp.where(row_id == i, total[:, i * lanes:(i + 1) * lanes], spread)
+    ext[0] = spread
+    ext_copy = remote(ext.at[0], ext_pair, p_s.at[2], p_r.at[2], core_peer)
+    ext_copy.start()
+    half32[...] = grad_half(rep)
+    hidv[...] = (pre * sig).astype(jnp.bfloat16)
+    store_hid = pltpu.make_async_copy(hidv, hid_out, loc_sem.at[4])
+    store_hid.start()
+
+    pair.wait()
+    ext_copy.wait()
+    both = half32[...] + pair_in[...].astype(jnp.float32)
+    half32[...] = both
+    half16[...] = both.astype(jnp.bfloat16)
+    ext[1] = ext[0] + ext_pair[...]
+    quarter = half_rows // PLANE
+    rs = []
+    for j in (3, 1, 2):
+        piece = half16.at[pl.ds(pl.multiple_of(flip(j) * quarter, quarter), quarter)]
+        rs.append(remote(piece, plane_in.at[j - 1], rs_s.at[j], rs_r.at[j], plane_peer[j]))
+        rs.append(remote(ext.at[1], ext_plane.at[j - 1], rs_s.at[j + 4], rs_r.at[j + 4], plane_peer[j]))
+    for c in rs:
+        c.start()
+    for c in rs:
+        c.wait()
+    part = half32[pl.ds(pl.multiple_of(q * quarter, quarter), quarter)]
+    for j in range(3):
+        part = part + plane_in[j].astype(jnp.float32)
+    sum32[...] = part
+    sum16[...] = part.astype(jnp.bfloat16)
+    ext[2] = ext[1] + (ext_plane[0] + ext_plane[1] + ext_plane[2])
+
+    share = quarter // Z
+    rs = []
+    for d in (2, 1, 3):
+        piece = sum16.at[pl.ds(pl.multiple_of(line(d) * share, share), share)]
+        rs.append(remote(piece, line_in.at[Z - d - 1], zl_s.at[d], zl_r.at[Z - d], line_peer[d]))
+        rs.append(remote(ext.at[2], ext_line.at[Z - d - 1], zl_s.at[d + 4], zl_r.at[Z - d + 4], line_peer[d]))
+    for c in rs:
+        c.start()
+    for c in rs:
+        c.wait()
+    part = sum32[pl.ds(pl.multiple_of(z * share, share), share)]
+    for d in range(3):
+        part = part + line_in[d].astype(jnp.float32)
+
+    def region(core, place, height, count):
+        start = core * half_rows + place * quarter + height * share
+        return fin.at[pl.ds(pl.multiple_of(start, share), count)]
+
+    here = region(rep, q, z, share)
+    here[...] = part.astype(jnp.bfloat16)
+
+    zg = [remote(here, here, zg_s.at[d], zg_r.at[Z - d], line_peer[d]) for d in (2, 1, 3)]
+    for c in zg:
+        c.start()
+    everything = ext[2] + (ext_line[0] + ext_line[1] + ext_line[2])
+    for i in range(4):
+        bias_out[:, i * lanes:(i + 1) * lanes] = everything[i:i + 1]
+    for c in zg:
+        c.wait()
+    mine_q = region(rep, q, 0, quarter)
+    pg = {j: remote(mine_q, mine_q, pg_s.at[j], pg_r.at[j], plane_peer[j]) for j in (3, 1, 2)}
+    for c in pg.values():
+        c.start()
+    cg = []
+    for j in (0, 1, 2, 3):
+        if j:
+            pg[j].wait_recv()
+        piece = region(rep, flip(j), 0, quarter)
+        cg.append(remote(piece, piece, cg_s.at[j], cg_r.at[j], core_peer))
+        cg[-1].start()
+    for c in cg:
+        c.wait()
+    store_wg = pltpu.make_async_copy(fin, wg_out, loc_sem.at[5])
+    store_wg.start()
+
+    for c in list(z_copy.values()) + list(x_copy.values()) + list(y_copy.values()) + list(dx_copy.values()) + list(dy_copy.values()) + list(pg.values()):
+        c.wait_send()
+    store_hid.wait()
+    store_wg.wait()
+
+
+def fused_shards(features, col_panels, block_counts, block_values, weight, bias, cotangent):
+    tile, width = features.shape
+    bf16, f32 = jnp.bfloat16, jnp.float32
+    half_rows = width // 2
+    quarter = half_rows // PLANE
+    share = quarter // Z
+    dma = pltpu.SemaphoreType.DMA
+    hbm = pl.BlockSpec(memory_space=pl.ANY)
+    smem = pl.BlockSpec(memory_space=pltpu.SMEM)
+    vmem = pl.BlockSpec(memory_space=pltpu.VMEM)
+    hidden, weight_sum, bias_sum = pl.pallas_call(
+        fused_kernel,
+        out_shape=(
+            jax.ShapeDtypeStruct((tile, width), bf16),
+            jax.ShapeDtypeStruct((width, width), bf16),
+            jax.ShapeDtypeStruct((1, width), f32),
+        ),
+        in_specs=[hbm, smem, smem, hbm, hbm, vmem, hbm],
+        out_specs=(hbm, hbm, vmem),
+        scratch_shapes=[
+            pltpu.VMEM((PLANE, Z * tile, width), bf16),
+            pltpu.VMEM((PLANE, 2 * tile, Z * tile), bf16),
+            pltpu.VMEM(block_values.shape, bf16),
+            pltpu.VMEM((width, width), bf16),
+            pltpu.VMEM((tile, width), bf16),
+            pltpu.VMEM((tile, width), f32),
+            pltpu.VMEM((tile, width), f32),
+            pltpu.VMEM((tile, width), f32),
+            pltpu.VMEM((tile, width), bf16),
+            pltpu.VMEM((tile, width), bf16),
+            pltpu.VMEM((half_rows, width), bf16),
+            pltpu.VMEM((half_rows, width), bf16),
+            pltpu.VMEM((half_rows, width), f32),
+            pltpu.VMEM((half_rows, width), bf16),
+            pltpu.VMEM((3, quarter, width), bf16),
+            pltpu.VMEM((quarter, width), f32),
+            pltpu.VMEM((quarter, width), bf16),
+            pltpu.VMEM((3, share, width), bf16),
+            pltpu.VMEM((width, width), bf16),
+            pltpu.VMEM((3, 8, width // 4), f32),
+            pltpu.VMEM((8, width // 4), f32),
+            pltpu.VMEM((3, 8, width // 4), f32),
+            pltpu.VMEM((3, 8, width // 4), f32),
+            dma((6,)),
+            dma((4,)), dma((4,)), dma((4,)), dma((4,)), dma((4,)), dma((4,)),
+            dma((4,)), dma((4,)), dma((4,)), dma((4,)),
+            dma((3,)), dma((3,)),
+            dma((8,)), dma((8,)), dma((8,)), dma((8,)),
+            dma((4,)), dma((4,)), dma((4,)), dma((4,)), dma((4,)), dma((4,)),
+        ],
+        compiler_params=pltpu.CompilerParams(
+            collective_id=0, has_side_effects=True, vmem_limit_bytes=32 * 1024 * 1024
+        ),
+        name="fused_layer",
+    )(features, col_panels, block_counts, block_values, weight, bias.reshape(1, width), cotangent)
+    factor = 1.0 / math.sqrt(lax.axis_size("section") * lax.axis_size("rep") * tile)
+    return hidden, weight_sum.astype(f32) * factor, bias_sum[0] * factor
+
+
+def fits_fused(mesh):
+    return dict(mesh.shape) == {"section": Z * PLANE, "rep": 2}
+
 
 def solution(mesh):
     in_specs = (
@@ -67,4 +360,5 @@
         P(("section", "rep"), None),
     )
     out_specs = (P(("section", "rep"), None), P(), P())
-    return jax.shard_map(shards, mesh=mesh, in_specs=in_specs, out_specs=out_specs, check_vma=False)
+    body = fused_shards if fits_fused(mesh) else shards
+    return jax.shard_map(body, mesh=mesh, in_specs=in_specs, out_specs=out_specs, check_vma=False)

time: 231 us -> 60.1 us (0.26)
  waiting for transfers between devices: 153 us -> 0 us
  Pallas kernels: 0 us -> 52.1 us
  blocking collectives: 43.4 us -> 0 us
  between operations: 14.8 us -> 0.66 us
  matrix products: 6.22 us -> 0 us
  other arithmetic: 5.83 us -> 1.69 us
    psum x1 -> x0, waiting for transfers between devices: 89.3 us -> none  [shards(): lax.psum((local_weight, local_bias), ('section', 'rep'))]
    all_gather x1 -> x0, waiting for transfers between devices: 62.9 us -> none  [shards(): gathered = lax.all_gather(features, 'section', axis=0, tiled=True)]
    pallas_call x0 -> x1, Pallas kernels: none -> 52.1 us  [fused_shards(): pl.pallas_call(fused_kernel, out_shape=(jax.ShapeDtypeStruct((tile, width...]
    psum x2 -> x0, blocking collectives: 43.4 us -> none  [the longest x1 38.5 us: shards(): lax.psum((local_weight, local_bias), ('section', 'rep'))]
    gather x3 -> x0, local copies, waits for them, and re-layouts: 6.61 us -> none  [one_turn(): picked = all_panels[step_cols]]
    dot_general x5 -> x0, matrix products: 6.22 us -> none  [the longest x3 3.92 us: one_turn(): jnp.einsum('gkab,gkbf->gaf', step_tiles, picked, preferred_element_type=j...]
    unnamed x6 -> x14, local copies, waits for them, and re-layouts: 0.02 us -> 5.4 us
  transfers between devices with their start and end apart: 2 -> 0, of which waited for: 2 -> 0; matrix products, arithmetic and copies ran while one was open for 1% -> 0% of each run, Pallas kernels for 0% -> 0%
where the time goes in v1:
time: 60.1 us; the launch traced here: 59.8 us
  Pallas kernels  52.1 us (87%)
  local copies, waits for them, and re-layouts  5.4 us (9%)
  other arithmetic  1.69 us (3%)
  between operations  0.66 us (1%)
    pallas_call x1, Pallas kernels, fused_shards(): pl.pallas_call(fused_kernel, out_shape=(jax.ShapeDtypeStruct((tile, width...  52.1 us
    unnamed x14, local copies, waits for them, and re-layouts  5.4 us
    mul x2, other arithmetic, fused_shards(): return (hidden, weight_sum.astype(f32) * factor, bias_sum[0] * factor)  1.69 us

profile of v1, /device:TPU:0, one launch (start us, length us, event | category | flops | bytes accessed | tf_op | source)
XLA Modules:
  0.0 59.8 jit_solution(16343124505735500045)
XLA Ops:
  0.6 0.0 copy-start.4
  0.6 0.0 copy-start.5
  0.7 0.8 %copy.10.counts = s32[2,1]{1,0:T(2,128)S(1)} copy(s32[2,1]{0,1:T(1,128)} %param.9) | data formatting | bytes 16 | tf_op args[2]
  1.4 0.0 copy-done.4
  1.4 0.0 copy-done.5
  1.4 0.0 copy-start
  1.4 1.1 %copy-done = bf16[2,1,12,128,128]{4,3,2,1,0:T(8,128)(2,1)S(1)} copy-done((bf16[2,1,12,128,128]{4,3,2,1,0:T(8,128)(2,1)S(1)}, bf16[2,1,12,128,128]{4,3,2,1,0:T(8,128)(2,1)}, u32[]{:S(2)}) %copy-start) | copy-done | bytes 786456
  2.5 0.0 copy-start.1
  2.5 1.0 %copy-done.1 = bf16[512,512]{1,0:T(8,128)(2,1)S(1)} copy-done((bf16[512,512]{1,0:T(8,128)(2,1)S(1)}, bf16[512,512]{1,0:T(8,128)(2,1)}, u32[]{:S(2)}) %copy-start.1) | copy-done | bytes 524312
  3.6 0.0 copy-start.2
  3.6 0.9 %copy-done.2 = bf16[128,512]{1,0:T(8,128)(2,1)S(1)} copy-done((bf16[128,512]{1,0:T(8,128)(2,1)S(1)}, bf16[128,512]{1,0:T(8,128)(2,1)}, u32[]{:S(2)}) %copy-start.2) | copy-done | bytes 131096
  4.5 0.0 copy-start.3
  4.5 0.9 %copy-done.3 = bf16[128,512]{1,0:T(8,128)(2,1)S(1)} copy-done((bf16[128,512]{1,0:T(8,128)(2,1)S(1)}, bf16[128,512]{1,0:T(8,128)(2,1)}, u32[]{:S(2)}) %copy-start.3) | copy-done | bytes 131096
  5.4 52.1 %fused_layer.1 = (bf16[128,512]{1,0:T(8,128)(2,1)S(1)}, bf16[512,512]{1,0:T(8,128)(2,1)S(1)}, f32[1,512]{1,0:T(1,128)S(1)}) custom-call(bf16[128,512]{1,0:T(8,128)(2,1)S(1)} %copy-done.2, s32[2,1,12]{2,1,0:T(1,128)S(1)} %copy-done.5, s32[2,1]{1,0:T(2,128)S(1)} %copy.10.counts, bf16[2,1,12,128,128]{4,3,2,1,0:T(8,128)(2,1)S(1)} %copy-done, ...), custom_call_target="tpu_custom_call" | custom-call | tf_op jit(solution)/shard_map/fused_layer/pallas_call | solution.py:299
  57.5 0.6 broadcast_multiply_fusion
  58.0 1.1 %convert_multiply_fusion = f32[512,512]{1,0:T(8,128)} fusion(bf16[512,512]{1,0:T(8,128)(2,1)S(1)} %get-tuple-element.7), kind=kLoop, calls=%fused_computation | loop fusion | flops 524288 | bytes 1572864 | tf_op jit(solution)/shard_map/mul | solution.py:345
  59.2 0.7 %copy.12 = bf16[128,512]{1,0:T(8,128)(2,1)} copy(bf16[128,512]{1,0:T(8,128)(2,1)S(1)} %get-tuple-element.12) | data formatting | bytes 262144
Async XLA Ops:
  0.6 0.8 %copy-start.4 = (f32[512]{0:T(512)S(1)}, f32[512]{0:T(512)}, u32[]{:S(2)}) copy-start(f32[512]{0:T(512)} %param.12) | copy-start | bytes 6148
  0.6 0.8 %copy-start.5 = (s32[2,1,12]{2,1,0:T(1,128)S(1)}, s32[2,1,12]{2,1,0:T(1,128)}, u32[]{:S(2)}) copy-start(s32[2,1,12]{2,1,0:T(1,128)} %cols.1) | copy-start | bytes 292
  1.4 1.1 %copy-start = (bf16[2,1,12,128,128]{4,3,2,1,0:T(8,128)(2,1)S(1)}, bf16[2,1,12,128,128]{4,3,2,1,0:T(8,128)(2,1)}, u32[]{:S(2)}) copy-start(bf16[2,1,12,128,128]{4,3,2,1,0:T(8,128)(2,1)} %blocks.1) | copy-start | bytes 2359300
  2.5 1.0 %copy-start.1 = (bf16[512,512]{1,0:T(8,128)(2,1)S(1)}, bf16[512,512]{1,0:T(8,128)(2,1)}, u32[]{:S(2)}) copy-start(bf16[512,512]{1,0:T(8,128)(2,1)} %weight.1) | copy-start | bytes 1572868
  3.6 0.9 %copy-start.2 = (bf16[128,512]{1,0:T(8,128)(2,1)S(1)}, bf16[128,512]{1,0:T(8,128)(2,1)}, u32[]{:S(2)}) copy-start(bf16[128,512]{1,0:T(8,128)(2,1)} %feat.1) | copy-start | bytes 393220
  4.5 0.9 %copy-start.3 = (bf16[128,512]{1,0:T(8,128)(2,1)S(1)}, bf16[128,512]{1,0:T(8,128)(2,1)}, u32[]{:S(2)}) copy-start(bf16[128,512]{1,0:T(8,128)(2,1)} %cot.1) | copy-start | bytes 393220
